TPU v7x, 256 devices: a whole 4x4x8 slice. The times are simulated.
256 devices in a mesh: group: 2 (over z_hi), dp: 8 (over x, core), tensor: 16 (over z_lo, y).
Axes of the slice: x: 4, y: 4, z: 8 (z_hi: 2, z_lo: 4; z = z_hi * 4 + z_lo), core: 2. Of those that a mesh axis runs over, the one named last changes fastest.
Arguments:
- teacher_hidden: bfloat16 [4096, 8192], P(('group', 'dp'), 'tensor'), may hold values from -6 to 6
- teacher_gain: float32 [8192], P('tensor'), may hold values from 0.1 to 1.9
- project_weight: bfloat16 [8192, 3584], P('tensor'), may hold values from -0.0625 to 0.0625
- student_hidden: bfloat16 [4096, 3584], P(('group', 'dp', 'tensor')), may hold values from -6 to 6
- student_gain: float32 [3584], replicated, may hold values from 0.1 to 1.9
- gate_weight: bfloat16 [3584, 9472], P(('group', 'dp'), 'tensor'), may hold values from -0.09375 to 0.09375
- up_weight: bfloat16 [3584, 9472], P(('group', 'dp'), 'tensor'), may hold values from -0.09375 to 0.09375
- down_weight: bfloat16 [9472, 3584], P('tensor', ('group', 'dp')), may hold values from -0.0625 to 0.0625
- owner_map: int32 [256, 1], P(('group', 'dp')), may hold values from 0 to 15; in each aligned block of 16 rows (0 to 15, 16 to 31, ...) at most 2 rows name the same one
- token_ids: int32 [4096], P(('group', 'dp', 'tensor')), may hold values from 0 to 511
- token_counts: int32 [256], P(('group', 'dp')), may hold values from 1 to 16
- id_weight: float32 [512], replicated, may hold values from 0.25 to 4
Outputs:
- student_out: bfloat16 [16, 16, 32, 3584], P(('group', 'dp'), 'tensor')
- down_grad: float32 [3584, 9472], P(('group', 'dp'), 'tensor')
Inputs may be any that keep to these rules, and one draw needn't show every extreme that they name: `owner_map`: of the 16 episodes of one index of group and dp (aligned blocks of 16 rows), at most 2 have the same owner; owner o is index o of group and dp in mesh order.
All inputs are finite; a program needn't handle non-finite values.
Results may differ from a plain program's by a relative error of at most 0.02.
Values may be sent and summed in bfloat16 or wider, within the bound.
No kernel may reach another device: no remote copies, remote signals or barrier semaphores. Data moves between devices by JAX's collectives and lax.ppermute only.
A program may use at most 128 MiB of HBM per device.

v0:
```python
import math
import jax
import jax.numpy as jnp
from jax import lax
from jax.sharding import Mesh
from jax.sharding import PartitionSpec as P

DT = 8192
EP_LEN = 16
TENSOR = ("tensor_0", "tensor_1")
OWNERS = ("group", "dp")
GROUP_DP_TENSOR = ("group", "dp", "tensor_0", "tensor_1")
EPSILON = 1e-06


def build_selector(owner_local, owners, capacity):
    owner = owner_local[:, 0]
    index = jnp.arange(owner.shape[0], dtype=jnp.int32)
    earlier = (owner[None, :] == owner[:, None]) & (index[None, :] < index[:, None])
    target = owner * capacity + jnp.sum(earlier.astype(jnp.int32), axis=1)
    slots = jnp.arange(owners * capacity, dtype=jnp.int32)
    return (target[None, :] == slots[:, None]).astype(jnp.bfloat16)


def local(
    teacher_hidden,
    teacher_gain,
    project_weight,
    student_hidden,
    student_gain,
    gate_weight,
    up_weight,
    down_weight,
    owner_map,
    token_ids,
    token_counts,
    id_weight,
):
    owners = lax.axis_size(OWNERS)
    episodes = token_counts.shape[0]
    capacity = max(2, 2 * episodes // owners)
    hidden = gate_weight.shape[1]
    position = lax.axis_index(TENSOR)
    tokens_all = EP_LEN * episodes * owners
    student = student_hidden.astype(jnp.float32)
    rescale = lax.rsqrt(jnp.mean(student * student, axis=1, keepdims=True) + EPSILON)
    normed = (student * rescale * student_gain[None, :]).astype(jnp.bfloat16)
    gathered = lax.all_gather(normed, TENSOR, axis=0, tiled=True)
    both = lax.all_gather(
        jnp.concatenate([gate_weight, up_weight], axis=1), OWNERS, axis=0, tiled=True
    )
    down = lax.all_gather(down_weight, OWNERS, axis=1, tiled=True)
    widened = teacher_hidden.astype(jnp.float32)
    squares = jnp.sum(widened * widened, axis=1)
    scaled = (widened * teacher_gain[None, :]).astype(jnp.bfloat16)
    totals = lax.psum_scatter(squares, TENSOR, scatter_dimension=0, tiled=True)
    inverse = lax.rsqrt(totals / DT + EPSILON)
    summed = lax.psum_scatter(
        jnp.dot(scaled, project_weight, preferred_element_type=jnp.float32).astype(jnp.bfloat16),
        TENSOR,
        scatter_dimension=0,
        tiled=True,
    ).astype(jnp.float32)
    projected = (summed * inverse[:, None]).astype(jnp.bfloat16).astype(jnp.float32)
    sums = jnp.dot(gathered, both, preferred_element_type=jnp.float32)
    activated = (jax.nn.silu(sums[:, :hidden]) * sums[:, hidden:]).astype(jnp.bfloat16)
    branch = jnp.dot(activated, down, preferred_element_type=jnp.float32).astype(jnp.bfloat16)
    branch_local = lax.psum_scatter(branch, TENSOR, scatter_dimension=0, tiled=True)
    predicted = student + branch_local.astype(jnp.float32)
    ids = jnp.arange(id_weight.shape[0], dtype=jnp.int32)
    looked = jnp.sum(jnp.where(token_ids[:, None] == ids[None, :], id_weight[None, :], 0.0), axis=1)
    weight = jnp.where(position < token_counts, looked, 0.0).astype(jnp.bfloat16)
    scale = 1.0 / math.sqrt(tokens_all)
    grad = (weight.astype(jnp.float32)[:, None] * (predicted - projected) * scale).astype(
        jnp.bfloat16
    )
    grad_all = lax.all_gather(grad, TENSOR, axis=0, tiled=True)
    down_grad = lax.psum_scatter(
        jnp.einsum("rc,rh->ch", grad_all, activated, preferred_element_type=jnp.float32).astype(
            jnp.bfloat16
        ),
        OWNERS,
        scatter_dimension=0,
        tiled=True,
    ).astype(jnp.float32)
    selector = build_selector(owner_map, owners, capacity)
    sent = jnp.dot(
        selector, predicted.astype(jnp.bfloat16), preferred_element_type=jnp.float32
    ).astype(jnp.bfloat16)
    student_out = lax.all_to_all(sent, OWNERS, 0, 0, tiled=True)
    return (student_out[None, None], down_grad)


def solution(mesh):
    split = Mesh(
        mesh.devices.reshape(mesh.shape["group"], mesh.shape["dp"], 4, 4),
        ("group", "dp", "tensor_0", "tensor_1"),
    )
    placed = (
        P(OWNERS, TENSOR),
        P(TENSOR),
        P(TENSOR, None),
        P(GROUP_DP_TENSOR, None),
        P(),
        P(OWNERS, TENSOR),
        P(OWNERS, TENSOR),
        P(TENSOR, OWNERS),
        P(OWNERS, None),
        P(GROUP_DP_TENSOR),
        P(OWNERS),
        P(),
    )
    return jax.shard_map(
        local,
        mesh=split,
        in_specs=placed,
        out_specs=(P(OWNERS, TENSOR, None, None), P(OWNERS, TENSOR)),
        check_vma=False,
    )
```

profile of v0, /device:TPU:8, one launch (start us, length us, event | category | flops | bytes accessed | tf_op | source)
XLA Modules:
  0.0 661.9 jit_solution(17144854641354540357)
XLA Ops:
  7.2 1.1 fusion.5
  8.3 1.6 fusion.7
  10.0 2.0 pad_maximum_fusion
  12.1 0.7 all-gather.9.cloned.1.call-update
  12.9 4.4 convolution_convert_fusion.2
  17.3 78.6 %all-gather.5.cloned.1.call-done = bf16[256,3584]{1,0:T(8,128)(2,1)} async-done(((bf16[16,3584]{1,0:T(8,128)(2,1)}), bf16[256,3584]{1,0:T(8,128)(2,1)}) %all-gather.5.cloned.1.call-update) | async-done | bytes 1835024 | tf_op jit(solution)/shard_map/all_gather | solution.py:48
  96.0 112.9 %all-gather.7.cloned.1.call-done = bf16[3584,1184]{1,0:T(8,128)(2,1)} async-done(((bf16[224,1184]{1,0:T(8,128)(2,1)}), bf16[3584,1184]{1,0:T(8,128)(2,1)}) %all-gather.7.cloned.1.call-update) | async-done | bytes 8486928 | tf_op jit(solution)/shard_map/all_gather | solution.py:49
  208.9 7.8 %fusion.16 = f32[256,1184]{0,1:T(8,128)S(1)} fusion(bf16[256,3584]{1,0:T(8,128)(2,1)} %all-gather.5.cloned.1.call-done, bf16[3584,1184]{1,0:T(8,128)(2,1)} %all-gather.7.cloned.1.call-done), kind=kOutput, calls=%fused_computation.36 | convolution fusion | flops 2172649472 | bytes 11534336 | tf_op jit(solution)/shard_map/dot_general | solution.py:65
  216.9 72.3 %all-gather.9.cloned.1.call-done = bf16[592,3584]{0,1:T(8,128)(2,1)} async-done(((bf16[592,224]{0,1:T(8,128)(2,1)}), bf16[592,3584]{0,1:T(8,128)(2,1)}) %all-gather.9.cloned.1.call-update) | async-done | bytes 4243472 | tf_op jit(solution)/shard_map/all_gather | solution.py:52
  289.1 5.2 convolution_convert_fusion.1
  294.4 0.6 copy-done.8
  295.0 0.6 dynamic-slice
  296.4 38.3 %all-reduce = f32[256]{0:T(256)S(1)} all-reduce(f32[256]{0:T(256)S(1)} %fusion.2), channel_id=4, replica_groups=mesh['group'=2,'dp'=8,'tensor_0'=4,'tensor_1'=4] {'tensor_0','tensor_1'}, use_global_device_ids=true, to_apply=%region_6.7.clone | all-reduce | flops 256 | bytes 2048
  335.0 35.2 %reduce-scatter.6.cloned.1.call-done = bf16[16,3584]{1,0:T(8,128)(2,1)} async-done(((bf16[256,3584]{1,0:T(8,128)(2,1)}), bf16[16,3584]{1,0:T(8,128)(2,1)}) %reduce-scatter.6.cloned.1.call-update) | async-done | bytes 114704 | tf_op jit(solution)/shard_map/reduce_scatter | solution.py:58
  370.2 86.1 %reduce-scatter.4.cloned.1.call-done = bf16[16,3584]{1,0:T(8,128)(2,1)} async-done(((bf16[256,3584]{1,0:T(8,128)(2,1)}), bf16[16,3584]{1,0:T(8,128)(2,1)}) %reduce-scatter.4.cloned.1.call-update) | async-done | bytes 114704 | tf_op jit(solution)/shard_map/reduce_scatter | solution.py:68
  456.3 1.7 multiply_convert_fusion
  458.1 83.8 %all-gather.11.cloned.1.call-done = bf16[256,3584]{1,0:T(8,128)(2,1)} async-done(((bf16[16,3584]{1,0:T(8,128)(2,1)}), bf16[256,3584]{1,0:T(8,128)(2,1)}) %all-gather.11.cloned.1.call-update) | async-done | bytes 1835024 | tf_op jit(solution)/shard_map/all_gather | solution.py:77
  541.8 5.2 convolution_convert_fusion
  547.1 0.6 copy-done.7
  548.0 0.2 convolution_convert_fusion.3
  548.3 18.0 %all_to_all.9 = bf16[16,2,3584]{2,1,0:T(2,128)(2,1)S(1)} all-to-all(bf16[16,2,3584]{2,1,0:T(2,128)(2,1)S(1)} %all_to_all.6), channel_id=1, replica_groups=mesh['group'=2,'dp'=8,'tensor_0'=4,'tensor_1'=4] {'group','dp'}, dimensions={0} | all-to-all | bytes 458752 | tf_op jit(solution)/shard_map/all_to_all | solution.py:90
  566.3 0.8 broadcast_in_dim.18
  567.1 86.2 %reduce-scatter.8.cloned.1.call-done = bf16[224,592]{1,0:T(8,128)(2,1)} async-done(((bf16[3584,592]{1,0:T(8,128)(2,1)}), bf16[224,592]{1,0:T(8,128)(2,1)}) %reduce-scatter.8.cloned.1.call-update) | async-done | bytes 265232 | tf_op jit(solution)/shard_map/reduce_scatter | solution.py:78
  653.2 1.8 convert_element_type.76
  (38 shorter events, 1.4 us)
Async XLA Ops:
  7.2 5.7 copy-start.1
  7.2 5.7 copy-start.3
  7.2 88.8 %all-gather.5.cloned.1.call-start = ((), (), s32[]{:S(2)}) async-start(), calls=%async_computation.4 | async-start | bytes 1949696 | tf_op jit(solution)/shard_map/all_gather | solution.py:48
  10.0 198.9 %all-gather.7.cloned.1.call-start = ((), (), s32[]{:S(2)}) async-start(), calls=%async_computation.5 | async-start | bytes 9748480 | tf_op jit(solution)/shard_map/all_gather | solution.py:49
  12.1 277.1 %all-gather.9.cloned.1.call-start = ((), (), s32[]{:S(2)}) async-start(), calls=%async_computation.6 | async-start | bytes 4874240 | tf_op jit(solution)/shard_map/all_gather | solution.py:52
  12.8 357.4 %reduce-scatter.6.cloned.1.call-start = ((), (), s32[]{:S(2)}) async-start(), calls=%async_computation.8 | async-start | bytes 1949696 | tf_op jit(solution)/shard_map/reduce_scatter | solution.py:58
  17.3 439.0 %reduce-scatter.4.cloned.1.call-start = ((), (), s32[]{:S(2)}) async-start(), calls=%async_computation.7 | async-start | bytes 1949696 | tf_op jit(solution)/shard_map/reduce_scatter | solution.py:68
  294.3 0.7 copy-start.8
  294.3 40.5 %copy-start.4 = (f32[512]{0:T(512)S(1)}, f32[512]{0:T(512)}, u32[]{:S(2)}) copy-start(f32[512]{0:T(512)} %param.23) | copy-start | bytes 6148
  294.3 40.5 %copy-start.5 = (s32[16]{0:T(128)S(1)}, s32[16]{0:T(128)}, u32[]{:S(2)}) copy-start(s32[16]{0:T(128)} %param.21) | copy-start | bytes 196
  294.3 40.7 %copy-start.6 = (s32[16]{0:T(128)S(1)}, s32[16]{0:T(128)}, u32[]{:S(2)}) copy-start(s32[16]{0:T(128)} %param.22) | copy-start | bytes 196
  294.4 161.9 %copy-start = (bf16[16,3584]{1,0:T(8,128)(2,1)S(1)}, bf16[16,3584]{1,0:T(8,128)(2,1)}, u32[]{:S(2)}) copy-start(bf16[16,3584]{1,0:T(8,128)(2,1)} %param.15) | copy-start | bytes 344068
  294.4 247.4 %all-gather.11.cloned.1.call-start = ((), (), s32[]{:S(2)}) async-start(), calls=%async_computation.9 | async-start | bytes 1949696 | tf_op jit(solution)/shard_map/all_gather | solution.py:77
  458.0 195.2 %reduce-scatter.8.cloned.1.call-start = ((), (), s32[]{:S(2)}) async-start(), calls=%async_computation.10 | async-start | bytes 4874240 | tf_op jit(solution)/shard_map/reduce_scatter | solution.py:78
  547.0 0.7 copy-start.7
  547.0 0.9 copy-start.2
Sparse Core Ops, SparseCore 0:
  10.4 85.5 all-gather.4
  99.3 109.5 all-gather.6
  211.6 77.4 all-gather.8
  291.5 78.5 reduce-scatter.5
  372.7 83.4 reduce-scatter.3
  458.5 83.3 all-gather.10
  547.2 106.0 reduce-scatter.7
where the time goes:
time: 662 us
  waiting for transfers between devices  556 us (84%)
  blocking collectives  56.4 us (9%)
  matrix products  22.8 us (3%)
  between operations  14.9 us (2%)
  other arithmetic  9.05 us (1%)
    all_gather x1, waiting for transfers between devices, local(): lax.all_gather(jnp.concatenate([gate_weight, up_weight], axis=1), OWNERS,...  113 us
    reduce_scatter x1, waiting for transfers between devices, local(): lax.psum_scatter(jnp.einsum('rc,rh->ch', grad_all, activated, preferred_e...  86.2 us
    reduce_scatter x1, waiting for transfers between devices, local(): lax.psum_scatter(branch, TENSOR, scatter_dimension=0, tiled=True)  86.1 us
    all_gather x1, waiting for transfers between devices, local(): grad_all = lax.all_gather(grad, TENSOR, axis=0, tiled=True)  83.8 us
    all_gather x1, waiting for transfers between devices, local(): gathered = lax.all_gather(normed, TENSOR, axis=0, tiled=True)  78.6 us
    all_gather x1, waiting for transfers between devices, local(): down = lax.all_gather(down_weight, OWNERS, axis=1, tiled=True)  72.3 us
    unnamed x1, blocking collectives  38.3 us
    reduce_scatter x1, waiting for transfers between devices, local(): lax.psum_scatter(jnp.dot(scaled, project_weight, preferred_element_type=j...  35.2 us
  transfers between devices with their start and end apart: 7, of which 7 were waited for; matrix products, arithmetic and copies ran while one was open for 3% of the time, Pallas kernels for 0%

commit v1 on v0

--- a/solution.py
+++ b/solution.py
@@ -11,6 +11,18 @@
 OWNERS = ("group", "dp")
 GROUP_DP_TENSOR = ("group", "dp", "tensor_0", "tensor_1")
 EPSILON = 1e-06
+
+
+def use_rates(page, dim_i):
+    return jnp.concatenate(
+        lax.all_to_all(
+            jnp.stack([page for _ in range(lax.axis_size(TENSOR))], 0),
+            axis_name=TENSOR,
+            split_axis=0,
+            concat_axis=0,
+        ),
+        dim_i,
+    )
 
 
 def build_selector(owner_local, owners, capacity):
@@ -74,7 +86,7 @@
     grad = (weight.astype(jnp.float32)[:, None] * (predicted - projected) * scale).astype(
         jnp.bfloat16
     )
-    grad_all = lax.all_gather(grad, TENSOR, axis=0, tiled=True)
+    grad_all = use_rates(grad, 0)
     down_grad = lax.psum_scatter(
         jnp.einsum("rc,rh->ch", grad_all, activated, preferred_element_type=jnp.float32).astype(
             jnp.bfloat16

time: 662 us -> 618 us (0.934)
  waiting for transfers between devices: 556 us -> 471 us
  blocking collectives: 56.4 us -> 97.9 us
    all_gather x1 -> x0, waiting for transfers between devices: 83.8 us -> none  [local(): grad_all = lax.all_gather(grad, TENSOR, axis=0, tiled=True)]
    all_to_all x0 -> x1, blocking collectives: none -> 39.9 us  [use_rates(): lax.all_to_all(jnp.stack([page for _ in range(lax.axis_size(TENSOR))], 0)...]
  transfers between devices with their start and end apart: 7 -> 6, of which waited for: 7 -> 6; matrix products, arithmetic and copies ran while one was open for 3% -> 4% of each run, Pallas kernels for 0% -> 0%
where the time goes in v1:
time: 618 us; the launch traced here: 617 us
  waiting for transfers between devices  471 us (76%)
  blocking collectives  97.9 us (16%)
  matrix products  21.3 us (3%)
  between operations  14.9 us (2%)
  other arithmetic  8.41 us (1%)
    all_gather x1, waiting for transfers between devices, local(): lax.all_gather(jnp.concatenate([gate_weight, up_weight], axis=1), OWNERS,...  113 us
    reduce_scatter x1, waiting for transfers between devices, local(): lax.psum_scatter(branch, TENSOR, scatter_dimension=0, tiled=True)  86 us
    reduce_scatter x1, waiting for transfers between devices, local(): lax.psum_scatter(jnp.einsum('rc,rh->ch', grad_all, activated, preferred_e...  85.7 us
    all_gather x1, waiting for transfers between devices, local(): gathered = lax.all_gather(normed, TENSOR, axis=0, tiled=True)  78.6 us
    all_gather x1, waiting for transfers between devices, local(): down = lax.all_gather(down_weight, OWNERS, axis=1, tiled=True)  72.3 us
    all_to_all x1, blocking collectives, use_rates(): lax.all_to_all(jnp.stack([page for _ in range(lax.axis_size(TENSOR))], 0)...  39.9 us
    unnamed x1, blocking collectives  38.4 us
    reduce_scatter x1, waiting for transfers between devices, local(): lax.psum_scatter(jnp.dot(scaled, project_weight, preferred_element_type=j...  35.1 us
  transfers between devices with their start and end apart: 6, of which 6 were waited for; matrix products, arithmetic and copies ran while one was open for 4% of the time, Pallas kernels for 0%

profile of v1, /device:TPU:8, one launch (start us, length us, event | category | flops | bytes accessed | tf_op | source)
XLA Modules:
  0.0 617.1 jit_solution(15536174703729178731)
XLA Ops:
  7.2 1.1 fusion.5
  8.3 1.6 fusion.7
  10.0 2.0 pad_maximum_fusion
  12.1 0.7 all-gather.8.cloned.1.call-update
  12.9 4.4 convolution_convert_fusion.2
  17.3 78.6 %all-gather.4.cloned.1.call-done = bf16[256,3584]{1,0:T(8,128)(2,1)} async-done(((bf16[16,3584]{1,0:T(8,128)(2,1)}), bf16[256,3584]{1,0:T(8,128)(2,1)}) %all-gather.4.cloned.1.call-update) | async-done | bytes 1835024 | tf_op jit(solution)/shard_map/all_gather | solution.py:60
  96.0 112.9 %all-gather.6.cloned.1.call-done = bf16[3584,1184]{1,0:T(8,128)(2,1)} async-done(((bf16[224,1184]{1,0:T(8,128)(2,1)}), bf16[3584,1184]{1,0:T(8,128)(2,1)}) %all-gather.6.cloned.1.call-update) | async-done | bytes 8486928 | tf_op jit(solution)/shard_map/all_gather | solution.py:61
  208.9 7.8 %fusion.16 = f32[256,1184]{0,1:T(8,128)S(1)} fusion(bf16[256,3584]{1,0:T(8,128)(2,1)} %all-gather.4.cloned.1.call-done, bf16[3584,1184]{1,0:T(8,128)(2,1)} %all-gather.6.cloned.1.call-done), kind=kOutput, calls=%fused_computation.36 | convolution fusion | flops 2172649472 | bytes 11534336 | tf_op jit(solution)/shard_map/dot_general | solution.py:77
  216.9 72.3 %all-gather.8.cloned.1.call-done = bf16[592,3584]{0,1:T(8,128)(2,1)} async-done(((bf16[592,224]{0,1:T(8,128)(2,1)}), bf16[592,3584]{0,1:T(8,128)(2,1)}) %all-gather.8.cloned.1.call-update) | async-done | bytes 4243472 | tf_op jit(solution)/shard_map/all_gather | solution.py:64
  289.1 5.2 convolution_convert_fusion.1
  294.5 0.6 copy-done.8
  295.0 0.6 dynamic-slice
  296.4 38.4 %all-reduce = f32[256]{0:T(256)S(1)} all-reduce(f32[256]{0:T(256)S(1)} %fusion.2), channel_id=4, replica_groups=mesh['group'=2,'dp'=8,'tensor_0'=4,'tensor_1'=4] {'tensor_0','tensor_1'}, use_global_device_ids=true, to_apply=%region_6.7.clone | all-reduce | flops 256 | bytes 2048
  335.1 35.1 %reduce-scatter.6.cloned.1.call-done = bf16[16,3584]{1,0:T(8,128)(2,1)} async-done(((bf16[256,3584]{1,0:T(8,128)(2,1)}), bf16[16,3584]{1,0:T(8,128)(2,1)}) %reduce-scatter.6.cloned.1.call-update) | async-done | bytes 114704 | tf_op jit(solution)/shard_map/reduce_scatter | solution.py:70
  370.2 86.0 %reduce-scatter.4.cloned.1.call-done = bf16[16,3584]{1,0:T(8,128)(2,1)} async-done(((bf16[256,3584]{1,0:T(8,128)(2,1)}), bf16[16,3584]{1,0:T(8,128)(2,1)}) %reduce-scatter.4.cloned.1.call-update) | async-done | bytes 114704 | tf_op jit(solution)/shard_map/reduce_scatter | solution.py:80
  456.2 1.1 multiply_convert_fusion
  457.5 39.9 %all_to_all.14 = bf16[16,16,3584]{2,1,0:T(8,128)(2,1)S(1)} all-to-all(bf16[16,16,3584]{2,1,0:T(8,128)(2,1)S(1)} %stack.2), channel_id=1, replica_groups=mesh['group'=2,'dp'=8,'tensor_0'=4,'tensor_1'=4] {'tensor_0','tensor_1'}, dimensions={0} | all-to-all | bytes 3670016 | tf_op jit(solution)/shard_map/all_to_all | solution.py:18
  497.4 3.7 convolution_convert_fusion
  501.1 0.6 copy-done.7
  502.0 0.2 convolution_convert_fusion.3
  502.3 19.6 %all_to_all.15 = bf16[16,2,3584]{2,1,0:T(2,128)(2,1)S(1)} all-to-all(bf16[16,2,3584]{2,1,0:T(2,128)(2,1)S(1)} %all_to_all.9), channel_id=1, replica_groups=mesh['group'=2,'dp'=8,'tensor_0'=4,'tensor_1'=4] {'group','dp'}, dimensions={0} | all-to-all | bytes 458752 | tf_op jit(solution)/shard_map/all_to_all | solution.py:102
  521.9 0.8 broadcast_in_dim.18
  522.7 85.7 %reduce-scatter.8.cloned.1.call-done = bf16[224,592]{1,0:T(8,128)(2,1)} async-done(((bf16[3584,592]{1,0:T(8,128)(2,1)}), bf16[224,592]{1,0:T(8,128)(2,1)}) %reduce-scatter.8.cloned.1.call-update) | async-done | bytes 265232 | tf_op jit(solution)/shard_map/reduce_scatter | solution.py:90
  608.4 1.8 convert_element_type.76
  (37 shorter events, 1.5 us)
Async XLA Ops:
  7.2 5.7 copy-start.1
  7.2 5.7 copy-start.3
  7.2 88.8 %all-gather.4.cloned.1.call-start = ((), (), s32[]{:S(2)}) async-start(), calls=%async_computation.5 | async-start | bytes 1949696 | tf_op jit(solution)/shard_map/all_gather | solution.py:60
  10.0 198.9 %all-gather.6.cloned.1.call-start = ((), (), s32[]{:S(2)}) async-start(), calls=%async_computation.6 | async-start | bytes 9748480 | tf_op jit(solution)/shard_map/all_gather | solution.py:61
  12.1 277.1 %all-gather.8.cloned.1.call-start = ((), (), s32[]{:S(2)}) async-start(), calls=%async_computation.7 | async-start | bytes 4874240 | tf_op jit(solution)/shard_map/all_gather | solution.py:64
  12.8 357.4 %reduce-scatter.6.cloned.1.call-start = ((), (), s32[]{:S(2)}) async-start(), calls=%async_computation.9 | async-start | bytes 1949696 | tf_op jit(solution)/shard_map/reduce_scatter | solution.py:70
  17.3 438.9 %reduce-scatter.4.cloned.1.call-start = ((), (), s32[]{:S(2)}) async-start(), calls=%async_computation.8 | async-start | bytes 1949696 | tf_op jit(solution)/shard_map/reduce_scatter | solution.py:80
  294.4 0.7 copy-start.8
  294.4 40.5 %copy-start.4 = (f32[512]{0:T(512)S(1)}, f32[512]{0:T(512)}, u32[]{:S(2)}) copy-start(f32[512]{0:T(512)} %param.23) | copy-start | bytes 6148
  294.4 40.5 %copy-start.5 = (s32[16]{0:T(128)S(1)}, s32[16]{0:T(128)}, u32[]{:S(2)}) copy-start(s32[16]{0:T(128)} %param.21) | copy-start | bytes 196
  294.4 40.7 %copy-start.6 = (s32[16]{0:T(128)S(1)}, s32[16]{0:T(128)}, u32[]{:S(2)}) copy-start(s32[16]{0:T(128)} %param.22) | copy-start | bytes 196
  294.4 161.8 %copy-start = (bf16[16,3584]{1,0:T(8,128)(2,1)S(1)}, bf16[16,3584]{1,0:T(8,128)(2,1)}, u32[]{:S(2)}) copy-start(bf16[16,3584]{1,0:T(8,128)(2,1)} %param.15) | copy-start | bytes 344068
  294.4 314.0 %reduce-scatter.8.cloned.1.call-start = ((), (), s32[]{:S(2)}) async-start(), calls=%async_computation.10 | async-start | bytes 4874240 | tf_op jit(solution)/shard_map/reduce_scatter | solution.py:90
  501.1 0.7 copy-start.7
  501.1 0.9 copy-start.2
Sparse Core Ops, SparseCore 0:
  10.4 85.5 all-gather.3
  99.3 109.5 all-gather.5
  211.6 77.4 all-gather.7
  291.5 78.6 reduce-scatter.5
  372.8 83.3 reduce-scatter.3
  501.2 107.1 reduce-scatter.7
